TPU v7x, 32 devices: a whole 2x2x4 slice. The times are simulated.
32 devices in a mesh: rows: 16 (over z, x, core), dirs: 2 (over y).
Axes of the slice: x: 2, y: 2, z: 4, core: 2. Of those that a mesh axis runs over, the one named last changes fastest.
Arguments:
- previous: bfloat16 [24, 32, 128, 512], P('dirs', None, 'rows'), may hold values from -12 to 12
- boundary: float32 [24, 32, 512], P('dirs'), may hold values from -6 to 6
- row_coupling: float32 [24, 128, 512], P('dirs', 'rows'), may hold values from 0 to 1
- cross_gain: float32 [24], P('dirs'), may hold values from 0.5 to 3
- block_inverse: float32 [24, 128, 128], P('dirs'), may hold values from 0 to 1, as said below
- quadrant: int32 [24], P('dirs'), may hold values from 0 to 3
- sea_mask: int32 [128, 512], P('rows'), may hold values from 0 to 1, as said below
- wet_tiles: int32 [128, 4], P('rows'), may hold values 0 or 1
- quad_coef: float32 [32], replicated, may hold values from 0.05 to 0.5
Outputs:
- action: bfloat16 [24, 32, 128, 512], P('dirs', None, 'rows')
Inputs may be any that keep to these rules, and one draw needn't show every extreme that they name: `sea_mask`: in each row the land cells, if any, are the last ones, from a coastline column to the end of the row. block_inverse[d] is the inverse of the 128 x 128 lower bidiagonal matrix with 1 + cross_gain[d] on its diagonal and -cross_gain[d] just below it.
All inputs are finite; a program needn't handle non-finite values. No bound on the sum of `wet_tiles` on one device may be relied on, other than what follows from the above.
Results may differ from a plain program's by a relative error of at most 0.0027.
Values may be sent and summed in bfloat16 or wider, within the bound.
A program may use at most 128 MiB of HBM per device.

v0:
```python
import jax
import jax.numpy as jnp
from jax import lax
from jax.sharding import PartitionSpec as P

SHIFT = 2
highest = lax.Precision.HIGHEST


def compose(preceding_part, following_part):
    return (
        following_part[0] * preceding_part[0],
        following_part[0] * preceding_part[1] + following_part[1],
    )


def higher_band(field):
    return jnp.concatenate([field[:, 1:], jnp.zeros_like(field[:, :1])], axis=1)


def lower_band(field):
    return jnp.concatenate([jnp.zeros_like(field[:, :1]), field[:, :-1]], axis=1)


def quad_terms(center, onward, against, coefficients):
    nonlinear = center * center * (onward + against) - 2.0 * center * onward * against
    return coefficients[None, :, None, None] * nonlinear


def full_source(spectra, coefficients):
    energy = spectra.astype(jnp.float32)
    onward = higher_band(jnp.roll(energy, -SHIFT, axis=0))
    against = lower_band(jnp.roll(energy, SHIFT, axis=0))
    return quad_terms(energy, onward, against, coefficients)


def on_device(
    previous,
    boundary,
    row_coupling,
    cross_gain,
    block_inverse,
    quadrant,
    sea_mask,
    wet_tiles,
    quad_coef,
):
    dir_dev, band_count, row_count, column_count = previous.shape
    block_size = block_inverse.shape[-1]
    sea_cells = sea_mask.astype(jnp.float32)
    backward = quadrant % 2 == 1
    sideways = quadrant // 2 == 1
    couple = row_coupling * sea_cells[None]
    forcing = sea_cells[None, None] * (1.0 - row_coupling)[:, None] * previous.astype(jnp.float32)
    couple = jnp.where(backward[:, None, None], jnp.flip(couple, 1), couple)
    forcing = jnp.where(backward[:, None, None, None], jnp.flip(forcing, 2), forcing)

    def row_step(carry, member):
        gain_now, value_now = carry
        gain_next = member[0][:, None] * gain_now
        value_next = member[0][:, None] * value_now + member[1]
        return ((gain_next, value_next), (gain_next, value_next))

    start_gain = jnp.ones((dir_dev, 1, column_count), jnp.float32)
    start_value = jnp.zeros((dir_dev, band_count, column_count), jnp.float32)
    last_maps, row_maps = lax.scan(
        row_step,
        (start_gain, start_value),
        (jnp.moveaxis(couple, 1, 0), jnp.moveaxis(forcing, 2, 0)),
    )
    span_gain = jnp.moveaxis(row_maps[0], 0, 2)
    partial_value = jnp.moveaxis(row_maps[1], 0, 2)
    block_gain, block_state = last_maps
    every_gain, every_state = (
        lax.all_gather(block_gain[None], "rows", axis=0, tiled=True),
        lax.all_gather(block_state[None], "rows", axis=0, tiled=True),
    )
    device_count = every_gain.shape[0]
    position = lax.axis_index("rows")
    order_flipping = backward[None, :, None, None]
    ordered_gain = jnp.where(order_flipping, jnp.flip(every_gain, 0), every_gain)
    ordered_state = jnp.where(order_flipping, jnp.flip(every_state, 0), every_state)

    def device_step(carry, member):
        return (compose(carry, member), carry)

    _, before_maps = lax.scan(
        device_step,
        (jnp.ones_like(block_gain), jnp.zeros_like(block_state)),
        (ordered_gain, ordered_state),
    )
    before_gain, before_state = before_maps
    onward_gain = lax.dynamic_index_in_dim(before_gain, position, 0, keepdims=False)
    onward_state = lax.dynamic_index_in_dim(before_state, position, 0, keepdims=False)
    against_gain = lax.dynamic_index_in_dim(
        before_gain, device_count - 1 - position, 0, keepdims=False
    )
    against_state = lax.dynamic_index_in_dim(
        before_state, device_count - 1 - position, 0, keepdims=False
    )
    inflow_gain = jnp.where(backward[:, None, None], against_gain, onward_gain)
    inflow_state = jnp.where(backward[:, None, None], against_state, onward_state)
    entering = inflow_gain * boundary + inflow_state
    swept_rows = partial_value + span_gain * entering[:, :, None, :]
    swept_rows = jnp.where(backward[:, None, None, None], jnp.flip(swept_rows, 2), swept_rows)
    flipped = jnp.where(sideways[:, None, None, None], jnp.flip(swept_rows, 3), swept_rows)
    blocks = flipped.reshape(dir_dev, band_count, row_count, column_count // block_size, block_size)
    solved = jnp.einsum(
        "dij,dfrkj->dfrki",
        block_inverse,
        blocks,
        precision=highest,
        preferred_element_type=jnp.float32,
    )
    first_column = block_inverse[:, :, 0][:, None, None, :]
    gain_column = cross_gain[:, None, None, None]
    pieces = [solved[:, :, :, 0]]
    for section in range(1, column_count // block_size):
        pieces.append(solved[:, :, :, section] + gain_column * pieces[-1][..., -1:] * first_column)
    settled = jnp.stack(pieces, 3).reshape(dir_dev, band_count, row_count, column_count)
    settled = (
        jnp.where(sideways[:, None, None, None], jnp.flip(settled, 3), settled)
        * sea_cells[None, None]
    )
    rounded = lax.optimization_barrier(settled.astype(jnp.bfloat16))
    gained = full_source(
        lax.all_to_all(rounded, "dirs", split_axis=2, concat_axis=0, tiled=True), quad_coef
    ).astype(jnp.bfloat16)
    returned = lax.all_to_all(gained, "dirs", split_axis=0, concat_axis=2, tiled=True)
    returned = lax.optimization_barrier(returned)
    wet_cells = jnp.repeat(wet_tiles.astype(jnp.float32), block_size, axis=1)
    return (settled + wet_cells[None, None] * returned.astype(jnp.float32)).astype(jnp.bfloat16)


def solution(mesh):
    in_specs = (
        P("dirs", None, "rows", None),
        P("dirs", None, None),
        P("dirs", "rows", None),
        P("dirs"),
        P("dirs", None, None),
        P("dirs"),
        P("rows", None),
        P("rows", None),
        P(),
    )
    out_specs = P("dirs", None, "rows", None)
    return jax.shard_map(
        on_device, mesh=mesh, in_specs=in_specs, out_specs=out_specs, check_vma=False
    )
```

profile of v0, /device:TPU:0, one launch (start us, length us, event | category | flops | bytes accessed | tf_op | source)
XLA Modules:
  0.0 633.3 jit_solution(5337060883751082020)
XLA Ops:
  8.9 5.4 convert_multiply_fusion
  14.3 11.2 %rev.27 = f32[12,32,8,512]{3,2,1,0:T(8,128)} reverse(f32[12,32,8,512]{3,2,1,0:T(8,128)} %convert_multiply_fusion), dimensions={2} | reverse | bytes 12582912 | tf_op jit(solution)/shard_map/jit(_flip)/rev | solution.py:56
  25.7 7.6 %select_bitcast_fusion = f32[8,12,32,512]{3,0,2,1:T(8,128)} fusion(f32[12,32,8,512]{3,2,1,0:T(8,128)} %rev.27, pred[12]{0:T(512)(128)(4,1)S(1)} %get-tuple-element.234, bf16[12,32,8,512]{3,2,1,0:T(8,128)(2,1)} %param.13, f32[12,8,512]{2,1,0:T(8,128)S(1)} %get-tuple-element.228), kind=kLoop, calls=%fused_computation.32 | loop fusion | flops 4718592 | bytes 15925260 | tf_op jit(solution)/shard_map/transpose | solution.py:69
  33.3 173.7 %while.34 = (s32[]{:T(128)}, f32[12,1,512]{2,1,0:T(1,128)S(1)}, f32[12,32,512]{2,1,0:T(8,128)S(1)}, f32[8,12,1,512]{3,0,1,2:T(8,128)S(1)}, f32[8,12,32,512]{3,0,...) while((s32[]{:T(128)}, f32[12,1,512]{2,1,0:T(1,128)S(1)}, ...), condition=%wide.region_1.2_spmd.clone, body=%wide.region_0.1_spmd.clone.sunk | while | flops 602115 | bytes 7299192 | solution.py:66
  33.4 3.7 constant_dynamic-slice_fusion.8
  38.3 16.7 %dynamic_update_slice.27 = f32[8,12,32,512]{3,0,2,1:T(8,128)} dynamic-update-slice(f32[8,12,32,512]{3,0,2,1:T(8,128)} %get-tuple-element.342, f32[1,12,32,512]{3,0,2,1:T(1,128)S(1)} %copy.159, s32[]{:T(128)} %get-tuple-element.338, s32[]{:T(128)} %constant.78.clone.1..sunk, s32[]{:T(128)} %constant.78.clone.1..sunk, s32[]{:T(128)} %constant.78.clone.1..sunk) | dynamic-update-slice | bytes 1572868 | tf_op jit(solution)/shard_map/while/body/jit(dynamic_update_index_in_dim)/dynamic_update_slice | solution.py:66
  55.2 3.6 constant_dynamic-slice_fusion.8
  60.0 16.7 %dynamic_update_slice.27 = f32[8,12,32,512]{3,0,2,1:T(8,128)} dynamic-update-slice(f32[8,12,32,512]{3,0,2,1:T(8,128)} %get-tuple-element.342, f32[1,12,32,512]{3,0,2,1:T(1,128)S(1)} %copy.159, s32[]{:T(128)} %get-tuple-element.338, s32[]{:T(128)} %constant.78.clone.1..sunk, s32[]{:T(128)} %constant.78.clone.1..sunk, s32[]{:T(128)} %constant.78.clone.1..sunk) | dynamic-update-slice | bytes 1572868 | tf_op jit(solution)/shard_map/while/body/jit(dynamic_update_index_in_dim)/dynamic_update_slice | solution.py:66
  76.9 3.6 constant_dynamic-slice_fusion.8
  81.7 16.7 %dynamic_update_slice.27 = f32[8,12,32,512]{3,0,2,1:T(8,128)} dynamic-update-slice(f32[8,12,32,512]{3,0,2,1:T(8,128)} %get-tuple-element.342, f32[1,12,32,512]{3,0,2,1:T(1,128)S(1)} %copy.159, s32[]{:T(128)} %get-tuple-element.338, s32[]{:T(128)} %constant.78.clone.1..sunk, s32[]{:T(128)} %constant.78.clone.1..sunk, s32[]{:T(128)} %constant.78.clone.1..sunk) | dynamic-update-slice | bytes 1572868 | tf_op jit(solution)/shard_map/while/body/jit(dynamic_update_index_in_dim)/dynamic_update_slice | solution.py:66
  98.6 3.6 constant_dynamic-slice_fusion.8
  103.4 16.7 %dynamic_update_slice.27 = f32[8,12,32,512]{3,0,2,1:T(8,128)} dynamic-update-slice(f32[8,12,32,512]{3,0,2,1:T(8,128)} %get-tuple-element.342, f32[1,12,32,512]{3,0,2,1:T(1,128)S(1)} %copy.159, s32[]{:T(128)} %get-tuple-element.338, s32[]{:T(128)} %constant.78.clone.1..sunk, s32[]{:T(128)} %constant.78.clone.1..sunk, s32[]{:T(128)} %constant.78.clone.1..sunk) | dynamic-update-slice | bytes 1572868 | tf_op jit(solution)/shard_map/while/body/jit(dynamic_update_index_in_dim)/dynamic_update_slice | solution.py:66
  120.3 3.6 constant_dynamic-slice_fusion.8
  125.1 16.7 %dynamic_update_slice.27 = f32[8,12,32,512]{3,0,2,1:T(8,128)} dynamic-update-slice(f32[8,12,32,512]{3,0,2,1:T(8,128)} %get-tuple-element.342, f32[1,12,32,512]{3,0,2,1:T(1,128)S(1)} %copy.159, s32[]{:T(128)} %get-tuple-element.338, s32[]{:T(128)} %constant.78.clone.1..sunk, s32[]{:T(128)} %constant.78.clone.1..sunk, s32[]{:T(128)} %constant.78.clone.1..sunk) | dynamic-update-slice | bytes 1572868 | tf_op jit(solution)/shard_map/while/body/jit(dynamic_update_index_in_dim)/dynamic_update_slice | solution.py:66
  142.0 3.6 constant_dynamic-slice_fusion.8
  146.8 16.7 %dynamic_update_slice.27 = f32[8,12,32,512]{3,0,2,1:T(8,128)} dynamic-update-slice(f32[8,12,32,512]{3,0,2,1:T(8,128)} %get-tuple-element.342, f32[1,12,32,512]{3,0,2,1:T(1,128)S(1)} %copy.159, s32[]{:T(128)} %get-tuple-element.338, s32[]{:T(128)} %constant.78.clone.1..sunk, s32[]{:T(128)} %constant.78.clone.1..sunk, s32[]{:T(128)} %constant.78.clone.1..sunk) | dynamic-update-slice | bytes 1572868 | tf_op jit(solution)/shard_map/while/body/jit(dynamic_update_index_in_dim)/dynamic_update_slice | solution.py:66
  163.7 3.6 constant_dynamic-slice_fusion.8
  168.5 16.7 %dynamic_update_slice.27 = f32[8,12,32,512]{3,0,2,1:T(8,128)} dynamic-update-slice(f32[8,12,32,512]{3,0,2,1:T(8,128)} %get-tuple-element.342, f32[1,12,32,512]{3,0,2,1:T(1,128)S(1)} %copy.159, s32[]{:T(128)} %get-tuple-element.338, s32[]{:T(128)} %constant.78.clone.1..sunk, s32[]{:T(128)} %constant.78.clone.1..sunk, s32[]{:T(128)} %constant.78.clone.1..sunk) | dynamic-update-slice | bytes 1572868 | tf_op jit(solution)/shard_map/while/body/jit(dynamic_update_index_in_dim)/dynamic_update_slice | solution.py:66
  185.4 3.6 constant_dynamic-slice_fusion.8
  190.3 16.7 %dynamic_update_slice.27 = f32[8,12,32,512]{3,0,2,1:T(8,128)} dynamic-update-slice(f32[8,12,32,512]{3,0,2,1:T(8,128)} %get-tuple-element.342, f32[1,12,32,512]{3,0,2,1:T(1,128)S(1)} %copy.159, s32[]{:T(128)} %get-tuple-element.338, s32[]{:T(128)} %constant.78.clone.1..sunk, s32[]{:T(128)} %constant.78.clone.1..sunk, s32[]{:T(128)} %constant.78.clone.1..sunk) | dynamic-update-slice | bytes 1572868 | tf_op jit(solution)/shard_map/while/body/jit(dynamic_update_index_in_dim)/dynamic_update_slice | solution.py:66
  208.4 25.4 %all-gather = f32[192,1,512]{2,1,0:T(1,128)S(1)} all-gather(f32[12,1,512]{2,1,0:T(1,128)S(1)} %get-tuple-element.85), channel_id=2, replica_groups=mesh['rows'=16,'dirs'=2] {'rows'}, dimensions={0}, use_global_device_ids=true | all-gather | bytes 417792 | tf_op jit(solution)/shard_map/all_gather | solution.py:75
  234.9 77.5 %all-gather.4.cloned.1.call-done = f32[192,32,512]{2,1,0:T(8,128)} async-done(((f32[12,32,512]{2,1,0:T(8,128)}), f32[192,32,512]{2,1,0:T(8,128)}) %all-gather.4.cloned.1.call-update) | async-done | bytes 12582928 | tf_op jit(solution)/shard_map/all_gather | solution.py:76
  312.4 17.5 %reverse_select_fusion = f32[16,12,32,512]{3,2,1,0:T(8,128)} fusion(f32[16,12,32,512]{3,2,1,0:T(8,128)} %bitcast.110, pred[12]{0:T(512)(128)(4,1)S(1)} %get-tuple-element.234), kind=kLoop, calls=%fused_computation.15 | loop fusion | flops 3145728 | bytes 25165836 | tf_op jit(solution)/shard_map/jit(_where)/select_n | solution.py:82
  329.9 61.8 %while.35 = (s32[]{:T(128)}, f32[12,1,512]{2,1,0:T(1,128)S(1)}, f32[12,32,512]{2,1,0:T(8,128)S(1)}, f32[16,12,1,512]{3,2,1,0:T(1,128)}, f32[16,12,32,512]{3,2,1,...) while((s32[]{:T(128)}, f32[12,1,512]{2,1,0:T(1,128)S(1)}, ...), condition=%wide.region_3.4_spmd.clone, body=%wide.region_2.3_spmd.clone.sunk | while | flops 804867 | bytes 4154482 | solution.py:87
  394.1 6.8 %bitcast_add_fusion.1 = f32[12,32,8,512]{3,2,1,0:T(8,128)} fusion(f32[8,12,32,512]{3,0,2,1:T(8,128)} %get-tuple-element.83, f32[12,32,512]{2,1,0:T(8,128)S(1)} %fusion.8, f32[12,8,512]{2,1,0:T(8,128)S(1)} %bitcast.118), kind=kLoop, calls=%fused_computation.24 | loop fusion | flops 3145728 | bytes 13565952 | tf_op jit(solution)/shard_map/add | solution.py:104
  400.8 11.2 %rev.30 = f32[12,32,8,512]{3,2,1,0:T(8,128)} reverse(f32[12,32,8,512]{3,2,1,0:T(8,128)} %bitcast_add_fusion.1), dimensions={2} | reverse | bytes 12582912 | tf_op jit(solution)/shard_map/jit(_flip)/rev | solution.py:105
  412.0 9.4 %broadcast_select_fusion.2 = f32[12,32,8,512]{3,2,1,0:T(8,128)} fusion(f32[12,32,8,512]{3,2,1,0:T(8,128)} %rev.30, pred[12]{0:T(512)(128)(4,1)S(1)} %get-tuple-element.234, f32[12,32,512]{2,1,0:T(8,128)S(1)} %fusion.8, f32[12,8,512]{2,1,0:T(8,128)S(1)} %bitcast.119, f32[8,12,32,512]{3,0,2,1:T(8,128)} %get-tuple-element.83), kind=kLoop, calls=%fused_computation.34 | loop fusion | flops 4718592 | bytes 19857420 | tf_op jit(solution)/shard_map/jit(_where)/select_n | solution.py:105
  421.5 12.5 %rev.31 = f32[12,32,8,512]{3,2,1,0:T(8,128)} reverse(f32[12,32,8,512]{3,2,1,0:T(8,128)} %broadcast_select_fusion.2), dimensions={3} | reverse | bytes 12582912 | tf_op jit(solution)/shard_map/jit(_flip)/rev | solution.py:106
  433.9 8.6 %fusion.2 = f32[12,32,8,4,128]{4,2,3,1,0:T(8,128)S(1)} fusion(f32[12,32,8,512]{3,2,1,0:T(8,128)} %rev.31, f32[12,32,8,512]{3,2,1,0:T(8,128)} %broadcast_select_fusion.2, pred[12]{0:T(512)(128)(4,1)S(1)} %get-tuple-element.233, f32[12,128,128]{2,1,0:T(8,128)S(1)} %copy-done.1), kind=kOutput, calls=%fused_computation.22 | convolution fusion | flops 2417491968 | bytes 19660812 | tf_op jit(solution)/shard_map/dij,dfrkj->dfrki/dot_general | solution.py:108
  442.5 2.5 fusion.18
  445.0 4.0 copy.136
  449.0 5.0 copy.137
  454.0 5.0 copy.139
  459.0 5.0 copy.140
  466.7 14.3 %multiply_add_fusion.2 = (f32[12,32,8,1,128]{1,2,4,0,3:T(8,128)}, f32[12,32,8,1,128]{1,2,4,0,3:T(8,128)}, f32[12,32,8,1,128]{1,2,4,0,3:T(8,128)}) fusion(f32[12,32,8,1,128]{1,2,4,0,3:T(8,128)} %copy.137, f32[12,128]{1,0:T(8,128)S(1)} %bitcast.121, f32[12,32,8]{1,2,0:T(8,128)S(1)} %fusion.13, f32[12,32,8,1,128]{1,2,4,0,3:T(8,128)} %copy.139, ...), kind=kLoop, calls=%fused_computation.30 | loop fusion | flops 2359296 | bytes 9480192 | tf_op jit(solution)/shard_map/add | solution.py:119
  481.1 5.5 copy.118
  486.6 5.5 copy.119
  492.1 5.5 copy.120
  497.6 4.4 maximum_bitcast_fusion
  502.0 12.5 %rev.32 = f32[12,32,8,512]{3,2,1,0:T(8,128)} reverse(f32[12,32,8,512]{3,2,1,0:T(8,128)} %maximum_bitcast_fusion), dimensions={3} | reverse | bytes 12582912 | tf_op jit(solution)/shard_map/jit(_flip)/rev | solution.py:122
  514.5 4.8 fusion.6
  520.3 39.4 %all_to_all.27 = bf16[12,32,8,512]{3,1,0,2:T(8,128)(2,1)S(1)} all-to-all(bf16[12,32,8,512]{3,1,0,2:T(8,128)(2,1)S(1)} %copy.121), channel_id=1, replica_groups=mesh['rows'=16,'dirs'=2] {'dirs'}, dimensions={2} | all-to-all | bytes 6291456 | tf_op jit(solution)/shard_map/all_to_all | solution.py:127
  561.8 5.7 fusion.17
  567.7 7.7 %multiply_convert_fusion = bf16[24,32,4,512]{3,1,2,0:T(8,128)(2,1)} fusion(f32[2,32,4,512]{3,1,2,0:T(8,128)S(1)} %get-tuple-element.219, f32[22,32,4,512]{3,1,2,0:T(8,128)} %get-tuple-element.221, f32[22,32,4,512]{3,1,2,0:T(8,128)} %get-tuple-element.220, f32[2,32,4,512]{3,1,2,0:T(8,128)S(1)} %get-tuple-element.218, f32[32]{0:T(128)S(1)} %copy-done.5, ...), kind=kLoop, calls=%fused_computation.26 | loop fusion | flops 26738688 | bytes 22020224 | tf_op jit(solution)/shard_map/convert_element_type | solution.py:128
  575.3 5.3 all-to-all-start.1
  580.8 35.9 %all-to-all-done.1 = bf16[24,32,4,512]{3,1,2,0:T(8,128)(2,1)} async-done(((bf16[24,32,4,512]{3,1,2,0:T(8,128)(2,1)}), bf16[24,32,4,512]{3,1,2,0:T(8,128)(2,1)}, u32[]{:S(2)}, u32[]{:S(2)}) %all-to-all-start.1) | async-done | bytes 3145760 | tf_op jit(solution)/shard_map/all_to_all | solution.py:129
  616.7 2.1 copy.124
  618.8 7.6 %add_convert_fusion = bf16[12,32,8,512]{3,2,1,0:T(8,128)(2,1)} fusion(bf16[12,32,8,512]{3,1,2,0:T(8,128)(2,1)S(1)} %bitcast.111, f32[8,512]{1,0:T(8,128)S(1)} %broadcast_bitcast_fusion, f32[8,512]{1,0:T(8,128)S(1)} %convert_element_type.33, f32[12,32,8,512]{3,2,1,0:T(8,128)} %rev.32, pred[12]{0:T(512)(128)(4,1)S(1)} %get-tuple-element.233, ...), kind=kLoop, calls=%fused_computation.25 | loop fusion | flops 14155776 | bytes 18907148 | tf_op jit(solution)/shard_map/convert_element_type | solution.py:132
  (163 shorter events, 85.7 us)
Async XLA Ops:
  6.5 305.9 %all-gather.4.cloned.1.call-start = ((), (), s32[]{:S(2)}) async-start(), calls=%async_computation.2 | async-start | bytes 13369344 | tf_op jit(solution)/shard_map/all_gather | solution.py:76
  33.3 174.7 %copy-start.1 = (f32[12,128,128]{2,1,0:T(8,128)S(1)}, f32[12,128,128]{2,1,0:T(8,128)}, u32[]{:S(2)}) copy-start(f32[12,128,128]{2,1,0:T(8,128)} %param.17) | copy-start | bytes 2359300
  207.1 0.9 copy-start
  329.9 62.6 %copy-start.2 = (f32[12,32,512]{2,1,0:T(8,128)S(1)}, f32[12,32,512]{2,1,0:T(8,128)}, u32[]{:S(2)}) copy-start(f32[12,32,512]{2,1,0:T(8,128)} %param.14) | copy-start | bytes 2359300
  454.0 10.1 %copy-start.3 = (f32[12]{0:T(128)S(1)}, f32[12]{0:T(128)}, u32[]{:S(2)}) copy-start(f32[12]{0:T(128)} %param.16) | copy-start | bytes 148
  561.8 5.8 copy-start.5
  575.3 5.3 copy-start.4
  575.3 41.4 %all-to-all-start.1 = ((bf16[24,32,4,512]{3,1,2,0:T(8,128)(2,1)}), bf16[24,32,4,512]{3,1,2,0:T(8,128)(2,1)}, u32[]{:S(2)}, u32[]{:S(2)}) async-start(bf16[24,32,4,512]{3,1,2,0:T(8,128)(2,1)} %multiply_convert_fusion), calls=%async_computation.1 | async-start | bytes 6291456 | tf_op jit(solution)/shard_map/all_to_all | solution.py:129
Sparse Core Ops, SparseCore 0:
  208.1 104.2 all-gather.3
where the time goes:
time: 641 us; the launch traced here: 633 us
  local copies, waits for them, and re-layouts  268 us (42%)
  other arithmetic  159 us (25%)
  waiting for transfers between devices  113 us (18%)
  blocking collectives  64.8 us (10%)
  between operations  13.6 us (2%)
  matrix products  8.55 us (1%)
    dynamic_update_slice x24, local copies, waits for them, and re-layouts, on_device(): lax.scan(row_step, (start_gain, start_value), (jnp.moveaxis(couple, 1, 0)...  141 us
    all_gather x1, waiting for transfers between devices, on_device(): lax.all_gather(block_state[None], 'rows', axis=0, tiled=True)  77.5 us
    all_to_all x1, blocking collectives, on_device(): lax.all_to_all(rounded, 'dirs', split_axis=2, concat_axis=0, tiled=True)  39.4 us
    all_to_all x1, waiting for transfers between devices, on_device(): lax.all_to_all(gained, 'dirs', split_axis=0, concat_axis=2, tiled=True)  35.9 us
    dynamic_slice x8, local copies, waits for them, and re-layouts, on_device(): lax.scan(row_step, (start_gain, start_value), (jnp.moveaxis(couple, 1, 0)...  29 us
    dynamic_update_slice x32, other arithmetic, on_device(): lax.scan(device_step, (jnp.ones_like(block_gain), jnp.zeros_like(block_st...  25.5 us
    all_gather x1, blocking collectives, on_device(): lax.all_gather(block_gain[None], 'rows', axis=0, tiled=True)  25.4 us
    add x16, other arithmetic, compose(): following_part[0] * preceding_part[1] + following_part[1]  23.1 us
  transfers between devices with their start and end apart: 2, of which 2 were waited for; matrix products, arithmetic and copies ran while one was open for 0% of the time, Pallas kernels for 0%

commit v1 on v0

--- a/solution.py
+++ b/solution.py
@@ -5,6 +5,18 @@
 
 SHIFT = 2
 highest = lax.Precision.HIGHEST
+
+
+def gather_by_bits(x, axis, dim):
+    ways, here, hop = (lax.axis_size(axis), lax.axis_index(axis), x.shape[dim])
+    line, have = (x, 1)
+    while have < ways:
+        line = jnp.concatenate(
+            [line, lax.ppermute(line, axis, [(d, (d - have) % ways) for d in range(ways)])],
+            axis=dim,
+        )
+        have = 2 * have
+    return jnp.roll(line, here * hop, axis=dim)
 
 
 def compose(preceding_part, following_part):
@@ -73,7 +85,7 @@
     block_gain, block_state = last_maps
     every_gain, every_state = (
         lax.all_gather(block_gain[None], "rows", axis=0, tiled=True),
-        lax.all_gather(block_state[None], "rows", axis=0, tiled=True),
+        gather_by_bits(block_state[None], "rows", 0),
     )
     device_count = every_gain.shape[0]
     position = lax.axis_index("rows")

time: 641 us -> 966 us (1.51)
  blocking collectives: 64.8 us -> 318 us
  local copies, waits for them, and re-layouts: 268 us -> 306 us
  waiting for transfers between devices: 113 us -> 150 us
  between operations: 13.6 us -> 0.23 us
    all_gather x1, blocking collectives: 25.4 us -> 278 us  [on_device(): lax.all_gather(block_gain[None], 'rows', axis=0, tiled=True)]
    ppermute x0 -> x4, waiting for transfers between devices: none -> 114 us  [gather_by_bits(): lax.ppermute(line, axis, [(d, (d - have) % ways) for d in range(ways)])]
    all_gather x1 -> x0, waiting for transfers between devices: 77.5 us -> none  [on_device(): lax.all_gather(block_state[None], 'rows', axis=0, tiled=True)]
    unnamed x17 -> x36, local copies, waits for them, and re-layouts: 20.3 us -> 40.1 us
    dynamic_slice x0 -> x1, local copies, waits for them, and re-layouts: none -> 12 us  [gather_by_bits(): return jnp.roll(line, here * hop, axis=dim)]
  transfers between devices with their start and end apart: 2 -> 5, of which waited for: 2 -> 4; matrix products, arithmetic and copies ran while one was open for 0% -> 1% of each run, Pallas kernels for 0% -> 0%
where the time goes in v1:
time: 966 us; the launch traced here: 958 us
  blocking collectives  318 us (33%)
  local copies, waits for them, and re-layouts  306 us (32%)
  other arithmetic  162 us (17%)
  waiting for transfers between devices  150 us (16%)
  starting transfers between devices  13 us (1%)
    all_gather x1, blocking collectives, on_device(): lax.all_gather(block_gain[None], 'rows', axis=0, tiled=True)  278 us
    dynamic_update_slice x24, local copies, waits for them, and re-layouts, on_device(): lax.scan(row_step, (start_gain, start_value), (jnp.moveaxis(couple, 1, 0)...  141 us
    ppermute x4, waiting for transfers between devices, gather_by_bits(): lax.ppermute(line, axis, [(d, (d - have) % ways) for d in range(ways)])  114 us
    unnamed x36, local copies, waits for them, and re-layouts  40.1 us
    all_to_all x1, blocking collectives, on_device(): lax.all_to_all(rounded, 'dirs', split_axis=2, concat_axis=0, tiled=True)  39.5 us
    all_to_all x1, waiting for transfers between devices, on_device(): lax.all_to_all(gained, 'dirs', split_axis=0, concat_axis=2, tiled=True)  36 us
    dynamic_slice x8, local copies, waits for them, and re-layouts, on_device(): lax.scan(row_step, (start_gain, start_value), (jnp.moveaxis(couple, 1, 0)...  28.9 us
    dynamic_update_slice x32, other arithmetic, on_device(): lax.scan(device_step, (jnp.ones_like(block_gain), jnp.zeros_like(block_st...  26.2 us
  transfers between devices with their start and end apart: 5, of which 4 were waited for; matrix products, arithmetic and copies ran while one was open for 1% of the time, Pallas kernels for 0%

profile of v1, /device:TPU:0, one launch (start us, length us, event | category | flops | bytes accessed | tf_op | source)
XLA Modules:
  0.0 958.0 jit_solution(5099604568214628415)
XLA Ops:
  2.4 5.4 convert_multiply_fusion
  7.8 11.2 %rev.27 = f32[12,32,8,512]{3,2,1,0:T(8,128)} reverse(f32[12,32,8,512]{3,2,1,0:T(8,128)} %convert_multiply_fusion), dimensions={2} | reverse | bytes 12582912 | tf_op jit(solution)/shard_map/jit(_flip)/rev | solution.py:68
  19.1 7.6 select_bitcast_fusion
  26.8 174.0 %while.34 = (s32[]{:T(128)}, f32[12,1,512]{2,1,0:T(1,128)S(1)}, f32[12,32,512]{2,1,0:T(8,128)S(1)}, f32[8,12,1,512]{3,0,1,2:T(8,128)S(1)}, f32[8,12,32,512]{3,0,...) while((s32[]{:T(128)}, f32[12,1,512]{2,1,0:T(1,128)S(1)}, ...), condition=%wide.region_1.2_spmd.clone, body=%wide.region_0.1_spmd.clone.sunk | while | flops 602115 | bytes 7299192 | solution.py:78
  26.9 3.6 constant_dynamic-slice_fusion.9
  31.7 16.7 %dynamic_update_slice.27 = f32[8,12,32,512]{3,0,2,1:T(8,128)} dynamic-update-slice(f32[8,12,32,512]{3,0,2,1:T(8,128)} %get-tuple-element.342, f32[1,12,32,512]{3,0,2,1:T(1,128)S(1)} %copy.159, s32[]{:T(128)} %get-tuple-element.338, s32[]{:T(128)} %constant.96.clone.1..sunk, s32[]{:T(128)} %constant.96.clone.1..sunk, s32[]{:T(128)} %constant.96.clone.1..sunk) | dynamic-update-slice | bytes 1572868 | tf_op jit(solution)/shard_map/while/body/jit(dynamic_update_index_in_dim)/dynamic_update_slice | solution.py:78
  48.6 3.6 constant_dynamic-slice_fusion.9
  53.5 16.7 %dynamic_update_slice.27 = f32[8,12,32,512]{3,0,2,1:T(8,128)} dynamic-update-slice(f32[8,12,32,512]{3,0,2,1:T(8,128)} %get-tuple-element.342, f32[1,12,32,512]{3,0,2,1:T(1,128)S(1)} %copy.159, s32[]{:T(128)} %get-tuple-element.338, s32[]{:T(128)} %constant.96.clone.1..sunk, s32[]{:T(128)} %constant.96.clone.1..sunk, s32[]{:T(128)} %constant.96.clone.1..sunk) | dynamic-update-slice | bytes 1572868 | tf_op jit(solution)/shard_map/while/body/jit(dynamic_update_index_in_dim)/dynamic_update_slice | solution.py:78
  75.2 16.7 %dynamic_update_slice.27 = f32[8,12,32,512]{3,0,2,1:T(8,128)} dynamic-update-slice(f32[8,12,32,512]{3,0,2,1:T(8,128)} %get-tuple-element.342, f32[1,12,32,512]{3,0,2,1:T(1,128)S(1)} %copy.159, s32[]{:T(128)} %get-tuple-element.338, s32[]{:T(128)} %constant.96.clone.1..sunk, s32[]{:T(128)} %constant.96.clone.1..sunk, s32[]{:T(128)} %constant.96.clone.1..sunk) | dynamic-update-slice | bytes 1572868 | tf_op jit(solution)/shard_map/while/body/jit(dynamic_update_index_in_dim)/dynamic_update_slice | solution.py:78
  97.0 16.7 %dynamic_update_slice.27 = f32[8,12,32,512]{3,0,2,1:T(8,128)} dynamic-update-slice(f32[8,12,32,512]{3,0,2,1:T(8,128)} %get-tuple-element.342, f32[1,12,32,512]{3,0,2,1:T(1,128)S(1)} %copy.159, s32[]{:T(128)} %get-tuple-element.338, s32[]{:T(128)} %constant.96.clone.1..sunk, s32[]{:T(128)} %constant.96.clone.1..sunk, s32[]{:T(128)} %constant.96.clone.1..sunk) | dynamic-update-slice | bytes 1572868 | tf_op jit(solution)/shard_map/while/body/jit(dynamic_update_index_in_dim)/dynamic_update_slice | solution.py:78
  118.7 16.7 %dynamic_update_slice.27 = f32[8,12,32,512]{3,0,2,1:T(8,128)} dynamic-update-slice(f32[8,12,32,512]{3,0,2,1:T(8,128)} %get-tuple-element.342, f32[1,12,32,512]{3,0,2,1:T(1,128)S(1)} %copy.159, s32[]{:T(128)} %get-tuple-element.338, s32[]{:T(128)} %constant.96.clone.1..sunk, s32[]{:T(128)} %constant.96.clone.1..sunk, s32[]{:T(128)} %constant.96.clone.1..sunk) | dynamic-update-slice | bytes 1572868 | tf_op jit(solution)/shard_map/while/body/jit(dynamic_update_index_in_dim)/dynamic_update_slice | solution.py:78
  140.4 16.7 %dynamic_update_slice.27 = f32[8,12,32,512]{3,0,2,1:T(8,128)} dynamic-update-slice(f32[8,12,32,512]{3,0,2,1:T(8,128)} %get-tuple-element.342, f32[1,12,32,512]{3,0,2,1:T(1,128)S(1)} %copy.159, s32[]{:T(128)} %get-tuple-element.338, s32[]{:T(128)} %constant.96.clone.1..sunk, s32[]{:T(128)} %constant.96.clone.1..sunk, s32[]{:T(128)} %constant.96.clone.1..sunk) | dynamic-update-slice | bytes 1572868 | tf_op jit(solution)/shard_map/while/body/jit(dynamic_update_index_in_dim)/dynamic_update_slice | solution.py:78
  157.4 3.6 constant_dynamic-slice_fusion.9
  162.2 16.7 %dynamic_update_slice.27 = f32[8,12,32,512]{3,0,2,1:T(8,128)} dynamic-update-slice(f32[8,12,32,512]{3,0,2,1:T(8,128)} %get-tuple-element.342, f32[1,12,32,512]{3,0,2,1:T(1,128)S(1)} %copy.159, s32[]{:T(128)} %get-tuple-element.338, s32[]{:T(128)} %constant.96.clone.1..sunk, s32[]{:T(128)} %constant.96.clone.1..sunk, s32[]{:T(128)} %constant.96.clone.1..sunk) | dynamic-update-slice | bytes 1572868 | tf_op jit(solution)/shard_map/while/body/jit(dynamic_update_index_in_dim)/dynamic_update_slice | solution.py:78
  179.1 3.6 constant_dynamic-slice_fusion.9
  183.9 16.7 %dynamic_update_slice.27 = f32[8,12,32,512]{3,0,2,1:T(8,128)} dynamic-update-slice(f32[8,12,32,512]{3,0,2,1:T(8,128)} %get-tuple-element.342, f32[1,12,32,512]{3,0,2,1:T(1,128)S(1)} %copy.159, s32[]{:T(128)} %get-tuple-element.338, s32[]{:T(128)} %constant.96.clone.1..sunk, s32[]{:T(128)} %constant.96.clone.1..sunk, s32[]{:T(128)} %constant.96.clone.1..sunk) | dynamic-update-slice | bytes 1572868 | tf_op jit(solution)/shard_map/while/body/jit(dynamic_update_index_in_dim)/dynamic_update_slice | solution.py:78
  200.8 5.5 collective-permute-start
  206.3 9.5 collective-permute-done
  216.6 34.2 %collective-permute-done.1 = f32[2,12,32,512]{3,2,1,0:T(8,128)S(1)} collective-permute-done((f32[2,12,32,512]{3,2,1,0:T(8,128)S(1)}, f32[2,12,32,512]{3,2,1,0:T(8,128)S(1)}, u32[]{:S(2)}, u32[]{:S(2)}) %collective-permute-start.1) | collective-permute-done | bytes 1572896 | tf_op jit(solution)/shard_map/ppermute | solution.py:15
  251.8 70.2 %collective-permute-done.2 = f32[4,12,32,512]{3,2,1,0:T(8,128)S(1)} collective-permute-done((f32[4,12,32,512]{3,2,1,0:T(8,128)S(1)}, f32[4,12,32,512]{3,2,1,0:T(8,128)S(1)}, u32[]{:S(2)}, u32[]{:S(2)}) %collective-permute-start.2) | collective-permute-done | bytes 3145760 | tf_op jit(solution)/shard_map/ppermute | solution.py:15
  329.3 278.3 %all-gather = f32[192,1,512]{2,1,0:T(1,128)S(1)} all-gather(f32[12,1,512]{2,1,0:T(1,128)S(1)} %get-tuple-element.85), channel_id=2, replica_groups=mesh['rows'=16,'dirs'=2] {'rows'}, dimensions={0}, use_global_device_ids=true | all-gather | bytes 417792 | tf_op jit(solution)/shard_map/all_gather | solution.py:87
  615.1 6.8 constant_dynamic-update-slice_fusion.5
  627.1 6.8 constant_dynamic-update-slice_fusion
  633.9 12.0 %constant_dynamic-slice_fusion.5 = f32[16,12,32,512]{3,2,1,0:T(8,128)} fusion(f32[32,12,32,512]{3,2,1,0:T(8,128)} %constant_dynamic-update-slice_fusion, s32[]{:T(128)S(6)} %select_n.78), kind=kLoop, calls=%fused_computation.71 | loop fusion | bytes 25165828 | tf_op jit(solution)/shard_map/jit(_roll_dynamic)/dynamic_slice | solution.py:19
  645.9 17.5 %reverse_select_fusion = f32[16,12,32,512]{3,2,1,0:T(8,128)} fusion(f32[16,12,32,512]{3,2,1,0:T(8,128)} %constant_dynamic-slice_fusion.5, pred[12]{0:T(512)(128)(4,1)S(1)} %get-tuple-element.234), kind=kLoop, calls=%fused_computation.15 | loop fusion | flops 3145728 | bytes 25165836 | tf_op jit(solution)/shard_map/jit(_where)/select_n | solution.py:94
  663.4 62.5 %while.35 = (s32[]{:T(128)}, f32[12,1,512]{2,1,0:T(1,128)S(1)}, f32[12,32,512]{2,1,0:T(8,128)S(1)}, f32[16,12,1,512]{3,2,1,0:T(1,128)}, f32[16,12,32,512]{3,2,1,...) while((s32[]{:T(128)}, f32[12,1,512]{2,1,0:T(1,128)S(1)}, ...), condition=%wide.region_3.4_spmd.clone, body=%wide.region_2.3_spmd.clone.sunk | while | flops 804867 | bytes 4154482 | solution.py:99
  728.2 6.7 bitcast_add_fusion.1
  735.0 11.2 %rev.30 = f32[12,32,8,512]{3,2,1,0:T(8,128)} reverse(f32[12,32,8,512]{3,2,1,0:T(8,128)} %bitcast_add_fusion.1), dimensions={2} | reverse | bytes 12582912 | tf_op jit(solution)/shard_map/jit(_flip)/rev | solution.py:117
  746.2 9.4 broadcast_select_fusion.2
  755.6 12.5 %rev.31 = f32[12,32,8,512]{3,2,1,0:T(8,128)} reverse(f32[12,32,8,512]{3,2,1,0:T(8,128)} %broadcast_select_fusion.2), dimensions={3} | reverse | bytes 12582912 | tf_op jit(solution)/shard_map/jit(_flip)/rev | solution.py:118
  768.1 8.6 fusion.2
  779.2 3.9 copy.136
  783.1 5.0 copy.137
  788.1 5.1 copy.139
  793.2 4.0 copy.140
  799.9 14.4 %multiply_add_fusion.2 = (f32[12,32,8,1,128]{1,2,4,0,3:T(8,128)}, f32[12,32,8,1,128]{1,2,4,0,3:T(8,128)}, f32[12,32,8,1,128]{1,2,4,0,3:T(8,128)}) fusion(f32[12,32,8,1,128]{1,2,4,0,3:T(8,128)} %copy.137, f32[12,128]{1,0:T(8,128)S(1)} %bitcast.126, f32[12,32,8]{1,2,0:T(8,128)S(1)} %fusion.13, f32[12,32,8,1,128]{1,2,4,0,3:T(8,128)} %copy.139, ...), kind=kLoop, calls=%fused_computation.31 | loop fusion | flops 2359296 | bytes 9480192 | tf_op jit(solution)/shard_map/add | solution.py:131
  814.3 4.4 copy.118
  818.7 5.5 copy.119
  824.2 5.5 copy.120
  829.8 4.2 maximum_bitcast_fusion
  834.0 12.4 %rev.32 = f32[12,32,8,512]{3,2,1,0:T(8,128)} reverse(f32[12,32,8,512]{3,2,1,0:T(8,128)} %maximum_bitcast_fusion), dimensions={3} | reverse | bytes 12582912 | tf_op jit(solution)/shard_map/jit(_flip)/rev | solution.py:134
  846.4 4.3 fusion.6
  851.8 39.5 %all_to_all.27 = bf16[12,32,8,512]{3,1,0,2:T(8,128)(2,1)S(1)} all-to-all(bf16[12,32,8,512]{3,1,0,2:T(8,128)(2,1)S(1)} %copy.121), channel_id=1, replica_groups=mesh['rows'=16,'dirs'=2] {'dirs'}, dimensions={2} | all-to-all | bytes 6291456 | tf_op jit(solution)/shard_map/all_to_all | solution.py:139
  893.4 5.8 fusion.17
  899.2 7.7 multiply_convert_fusion
  906.9 5.3 all-to-all-start.1
  912.3 36.0 %all-to-all-done.1 = bf16[24,32,4,512]{3,1,2,0:T(8,128)(2,1)} async-done(((bf16[24,32,4,512]{3,1,2,0:T(8,128)(2,1)}), bf16[24,32,4,512]{3,1,2,0:T(8,128)(2,1)}, u32[]{:S(2)}, u32[]{:S(2)}) %all-to-all-start.1) | async-done | bytes 3145760 | tf_op jit(solution)/shard_map/all_to_all | solution.py:141
  951.2 6.9 add_convert_fusion
  (192 shorter events, 125.7 us)
Async XLA Ops:
  200.8 15.0 %collective-permute-start = (f32[1,12,32,512]{3,2,1,0:T(8,128)S(1)}, f32[1,12,32,512]{3,2,1,0:T(8,128)S(1)}, u32[]{:S(2)}, u32[]{:S(2)}) collective-permute-start(f32[1,12,32,512]{3,2,1,0:T(8,128)S(1)} %bitcast.107), channel_id=1, source_target_pairs={{0,30},{2,0},{4,2},{6,4},{8,6},{10,8},{12,10},{14,12},{16,14},{18,... | collective-permute-start | bytes 2359304 | tf_op jit(solution)/shard_map/ppermute | solution.py:15
  215.8 111.0 %copy-start.4 = (f32[1,12,32,512]{3,2,1,0:T(8,128)}, f32[1,12,32,512]{3,2,1,0:T(8,128)S(1)}, u32[]{:S(2)}) copy-start(f32[1,12,32,512]{3,2,1,0:T(8,128)S(1)} %collective-permute-done) | copy-start | bytes 2359300
  216.0 34.8 %collective-permute-start.1 = (f32[2,12,32,512]{3,2,1,0:T(8,128)S(1)}, f32[2,12,32,512]{3,2,1,0:T(8,128)S(1)}, u32[]{:S(2)}, u32[]{:S(2)}) collective-permute-start(f32[2,12,32,512]{3,2,1,0:T(8,128)S(1)} %pad_maximum_fusion.2), channel_id=1, source_target_pairs={{0,28},{2,30},{4,0},{6,2},{8,4},{10,6},{12,8},{14,10},{16,12},{18,... | collective-permute-start | bytes 4718600 | tf_op jit(solution)/shard_map/ppermute | solution.py:15
  251.3 70.8 %collective-permute-start.2 = (f32[4,12,32,512]{3,2,1,0:T(8,128)S(1)}, f32[4,12,32,512]{3,2,1,0:T(8,128)S(1)}, u32[]{:S(2)}, u32[]{:S(2)}) collective-permute-start(f32[4,12,32,512]{3,2,1,0:T(8,128)S(1)} %pad_maximum_fusion.1), channel_id=1, source_target_pairs={{0,24},{2,26},{4,28},{6,30},{8,0},{10,2},{12,4},{14,6},{16,8},{18,... | collective-permute-start | bytes 9437192 | tf_op jit(solution)/shard_map/ppermute | solution.py:15
  322.1 1.7 copy-start
  326.7 288.3 %collective-permute-start.3 = (f32[8,12,32,512]{3,2,1,0:T(8,128)}, f32[8,12,32,512]{3,2,1,0:T(8,128)}, u32[]{:S(2)}, u32[]{:S(2)}) collective-permute-start(f32[8,12,32,512]{3,2,1,0:T(8,128)} %pad_maximum_fusion), channel_id=1, source_target_pairs={{0,16},{2,18},{4,20},{6,22},{8,24},{10,26},{12,28},{14,30},{16,0},... | collective-permute-start | bytes 18874376 | tf_op jit(solution)/shard_map/ppermute | solution.py:15
  329.3 283.8 %copy-start.1 = (f32[4,12,32,512]{3,2,1,0:T(8,128)S(1)}, f32[4,12,32,512]{3,2,1,0:T(8,128)}, u32[]{:S(2)}) copy-start(f32[4,12,32,512]{3,2,1,0:T(8,128)} %copy-done) | copy-start | bytes 9437188
  615.1 7.8 copy-start.5
  663.4 63.3 %copy-start.7 = (f32[12,32,512]{2,1,0:T(8,128)S(1)}, f32[12,32,512]{2,1,0:T(8,128)}, u32[]{:S(2)}) copy-start(f32[12,32,512]{2,1,0:T(8,128)} %param.14) | copy-start | bytes 2359300
  755.6 12.5 %copy-start.6 = (f32[12,128,128]{2,1,0:T(8,128)S(1)}, f32[12,128,128]{2,1,0:T(8,128)}, u32[]{:S(2)}) copy-start(f32[12,128,128]{2,1,0:T(8,128)} %param.17) | copy-start | bytes 2359300
  788.1 9.1 copy-start.8
  893.4 5.9 copy-start.10
  906.9 5.3 copy-start.9
  906.9 41.5 %all-to-all-start.1 = ((bf16[24,32,4,512]{3,1,2,0:T(8,128)(2,1)}), bf16[24,32,4,512]{3,1,2,0:T(8,128)(2,1)}, u32[]{:S(2)}, u32[]{:S(2)}) async-start(bf16[24,32,4,512]{3,1,2,0:T(8,128)(2,1)} %multiply_convert_fusion), calls=%async_computation.1 | async-start | bytes 6291456 | tf_op jit(solution)/shard_map/all_to_all | solution.py:141
  948.4 2.4 copy-start.2
  948.4 2.8 copy-start.3
